TPU v7x, 32 devices: a whole 2x2x4 slice. The times are simulated.
32 devices in a mesh: seq: 8 (over y, x, core), sub: 4 (over z).
Axes of the slice: x: 2, y: 2, z: 4, core: 2. Of those that a mesh axis runs over, the one named last changes fastest.
Arguments:
- activations: bfloat16 [4096, 1024], P(('seq', 'sub')), may hold values from -6 to 6
- conv_weight: bfloat16 [5, 1152, 1024], P(None, 'sub'), may hold values from -1 to 1
- cotangent: bfloat16 [1024, 1152], P('seq', 'sub'), may hold values from -6 to 6
Outputs:
- features: bfloat16 [1024, 1152], P('seq', 'sub')
- input_grad: bfloat16 [4096, 1024], P(('seq', 'sub'))
- weight_grad: float32 [1024, 5, 1152], P('seq', None, 'sub')
All inputs are finite; a program needn't handle non-finite values.
Results may differ from a plain program's by a relative error of at most 0.02.
Values may be sent and summed in bfloat16 or wider, within the bound.
A program may use at most 64 MiB of HBM per device.

v0:
```python
import jax
import jax.numpy as jnp
from jax import lax
from jax.sharding import PartitionSpec as P

EPSILON = 1e-06


def padded_2(block, sides, width):
    for axis, dim in sides:
        count = lax.axis_size(axis)
        forward = [(i, i + 1) for i in range(count - 1)]
        backward = [(target, source) for source, target in forward]
        low = lax.ppermute(
            lax.slice_in_dim(block, block.shape[dim] - width, None, axis=dim), axis, forward
        )
        high = lax.ppermute(lax.slice_in_dim(block, 0, width, axis=dim), axis, backward)
        block = jnp.concatenate([low, block, high], axis=dim)
    return block


def gelu_slope(tensor):
    return (
        0.5 * (1.0 + jax.scipy.special.erf(tensor * 0.7071067811865476))
        + tensor * jnp.exp(-0.5 * tensor * tensor) * 0.3989422804014327
    )


def pool_pairs(tensor):
    half_rows = tensor.shape[0] // 2
    return 0.5 * jnp.sum(tensor.reshape(half_rows, 2, tensor.shape[1]), axis=1)


def per_device(activations, conv_weight, cotangent):
    tap_count = conv_weight.shape[0]
    in_width = activations.shape[1]
    out_width = conv_weight.shape[1]
    full_out = out_width * lax.axis_size("sub")
    x_float = activations.astype(jnp.float32)
    inv_first = lax.rsqrt(jnp.mean(x_float * x_float, axis=1, keepdims=True) + EPSILON)
    normed_first = x_float * inv_first
    pooled = pool_pairs(jax.nn.gelu(normed_first, approximate=False)).astype(jnp.bfloat16)
    gathered = lax.all_gather(pooled, "sub", axis=0, tiled=True)
    block_rows = gathered.shape[0]
    padded = padded_2(gathered, (("seq", 0),), 2)
    conv_acc = jnp.zeros((block_rows, out_width), jnp.float32)
    for offset in range(tap_count):
        conv_acc = conv_acc + lax.dot_general(
            padded[offset : offset + block_rows],
            conv_weight[offset],
            (((1,), (1,)), ((), ())),
            preferred_element_type=jnp.float32,
        )
    conv_out = conv_acc.astype(jnp.bfloat16)
    y_float = conv_out.astype(jnp.float32)
    square_sum = lax.psum(jnp.sum(y_float * y_float, axis=1), "sub")
    inv_second = lax.rsqrt(square_sum / full_out + EPSILON)[:, None]
    normed_second = y_float * inv_second
    features = pool_pairs(jax.nn.gelu(normed_second, approximate=False)).astype(jnp.bfloat16)
    upstream = 0.5 * jnp.repeat(cotangent.astype(jnp.float32), 2, axis=0)
    slope_second = upstream * gelu_slope(normed_second)
    inner_second = lax.psum(jnp.sum(slope_second * normed_second, axis=1), "sub")
    conv_grad = (
        inv_second * (slope_second - normed_second * (inner_second / full_out)[:, None])
    ).astype(jnp.bfloat16)
    grad_padded = padded_2(conv_grad, (("seq", 0),), 2)
    running = jnp.zeros((block_rows, in_width), jnp.float32)
    for offset in range(tap_count):
        window = lax.dynamic_slice_in_dim(grad_padded, 0 + 4 - offset, block_rows, 0)
        running = running + jnp.dot(window, conv_weight[offset], preferred_element_type=jnp.float32)
    owned = lax.psum_scatter(
        running.astype(jnp.bfloat16), "sub", scatter_dimension=1, tiled=True
    ).astype(jnp.float32)
    pooled_grad = lax.all_to_all(
        owned.astype(jnp.bfloat16), "sub", split_axis=0, concat_axis=1, tiled=True
    ).astype(owned.dtype)
    slope_first = 0.5 * jnp.repeat(pooled_grad, 2, axis=0) * gelu_slope(normed_first)
    inner_first = jnp.mean(slope_first * normed_first, axis=1, keepdims=True)
    input_grad = (inv_first * (slope_first - normed_first * inner_first)).astype(jnp.bfloat16)
    pieces = [
        lax.dot_general(
            padded[offset : offset + block_rows],
            conv_grad,
            (((0,), (0,)), ((), ())),
            preferred_element_type=jnp.float32,
        )
        for offset in range(tap_count)
    ]
    weight_grad = lax.psum_scatter(
        jnp.stack(pieces, axis=1).astype(jnp.bfloat16), "seq", scatter_dimension=0, tiled=True
    ).astype(jnp.float32)
    return (features, input_grad, weight_grad)


def solution(mesh):
    return jax.shard_map(
        per_device,
        mesh=mesh,
        in_specs=(P(("seq", "sub"), None), P(None, "sub", None), P("seq", "sub")),
        out_specs=(P("seq", "sub"), P(("seq", "sub"), None), P("seq", None, "sub")),
        check_vma=False,
    )
```

profile of v0, /device:TPU:1, one launch (start us, length us, event | category | flops | bytes accessed | tf_op | source)
XLA Modules:
  0.0 169.4 jit_solution(15524808999855890271)
XLA Ops:
  7.2 1.2 fusion.78
  8.5 3.0 %fusion.40 = f32[128,1024]{1,0:T(8,128)} fusion(bf16[128,1024]{1,0:T(8,128)(2,1)} %param.3, f32[128]{0:T(128)S(1)} %add_rsqrt_fusion.1), kind=kLoop, calls=%fused_computation.55 | loop fusion | flops 8650752 | bytes 786944 | tf_op jit(solution)/shard_map/mul | solution.py:42
  11.4 1.3 reshape.38
  12.8 1.3 reduce_sum.55
  14.1 1.0 multiply_convert_fusion.1
  15.1 15.3 %all_gather.3 = bf16[256,1024]{1,0:T(8,128)(2,1)S(1)} all-gather(bf16[64,1024]{1,0:T(8,128)(2,1)S(1)} %multiply_convert_fusion.1), channel_id=1, replica_groups=mesh['seq'=8,'sub'=4] {'sub'}, dimensions={0}, use_global_device_ids=true | all-gather | bytes 655360 | tf_op jit(solution)/shard_map/all_gather | solution.py:43
  30.4 0.6 fusion.124
  31.0 5.1 %collective-permute-start = (bf16[2,1024]{1,0:T(2,128)(2,1)}, bf16[2,1024]{1,0:T(2,128)(2,1)}, u32[]{:S(2)}, u32[]{:S(2)}) collective-permute-start(bf16[2,1024]{1,0:T(2,128)(2,1)} %get-tuple-element.10), channel_id=1, source_target_pairs={{0,4},{4,8},{8,12},{12,16},{16,20},{20,24},{24,28},{1,5},{5,9},{9,... | collective-permute-start | bytes 12296 | tf_op jit(solution)/shard_map/ppermute | solution.py:14
  36.1 1.9 %collective-permute-start.1 = (bf16[2,1024]{1,0:T(2,128)(2,1)}, bf16[2,1024]{1,0:T(2,128)(2,1)S(1)}, u32[]{:S(2)}, u32[]{:S(2)}) collective-permute-start(bf16[2,1024]{1,0:T(2,128)(2,1)} %get-tuple-element.11), channel_id=1, source_target_pairs={{4,0},{8,4},{12,8},{16,12},{20,16},{24,20},{28,24},{5,1},{9,5},{13... | collective-permute-start | bytes 12296 | tf_op jit(solution)/shard_map/ppermute | solution.py:17
  38.0 1.1 fusion.31
  39.1 0.8 copy.11
  39.9 0.9 convert_multiply_fusion.2
  40.8 0.8 constant_dynamic-update-slice_fusion.1
  41.6 0.9 broadcast_in_dim.4
  42.5 2.0 %mul.177 = f32[256,288]{1,0:T(8,128)} reshape(f32[128,2,288]{2,1,0:T(2,128)} %broadcast_in_dim.4) | data formatting | bytes 589824 | tf_op jit(solution)/shard_map/mul | solution.py:60
  44.5 1.9 %copy.12 = f32[256,288]{0,1:T(8,128)} copy(f32[256,288]{1,0:T(8,128)} %mul.177) | data formatting | bytes 589824 | tf_op jit(solution)/shard_map/mul | solution.py:60
  46.4 0.6 constant_dynamic-update-slice_fusion
  47.0 1.5 fusion.25
  48.5 1.0 fusion.35
  49.5 1.0 fusion.14
  50.6 1.1 multiply_reduce_fusion.1
  51.7 10.4 %psum.14 = f32[256]{0:T(256)S(1)} all-reduce(f32[256]{0:T(256)S(1)} %get-tuple-element.16), channel_id=1, replica_groups=mesh['seq'=8,'sub'=4] {'sub'}, use_global_device_ids=true, to_apply=%region_3.0 | all-reduce | flops 256 | bytes 2048 | tf_op jit(solution)/shard_map/psum | solution.py:56
  62.1 1.2 multiply_reduce_fusion
  63.3 6.6 %psum.15 = f32[256]{0:T(256)S(1)} all-reduce(f32[256]{0:T(256)S(1)} %get-tuple-element.8), channel_id=1, replica_groups=mesh['seq'=8,'sub'=4] {'sub'}, use_global_device_ids=true, to_apply=%region_6.0 | all-reduce | flops 256 | bytes 2048 | tf_op jit(solution)/shard_map/psum | solution.py:62
  69.9 1.6 multiply_convert_fusion
  71.7 3.9 %collective-permute-start.2 = (bf16[2,288]{0,1:T(8,128)(2,1)S(1)}, bf16[2,288]{0,1:T(8,128)(2,1)S(1)}, u32[]{:S(2)}, u32[]{:S(2)}) collective-permute-start(bf16[2,288]{0,1:T(8,128)(2,1)S(1)} %get-tuple-element.14), channel_id=1, source_target_pairs={{4,0},{8,4},{12,8},{16,12},{20,16},{24,20},{28,24},{5,1},{9,5},{13... | collective-permute-start | bytes 3464 | tf_op jit(solution)/shard_map/ppermute | solution.py:17
  75.6 1.5 fusion.29
  77.1 5.4 %collective-permute-start.3 = (bf16[2,288]{0,1:T(8,128)(2,1)S(1)}, bf16[2,288]{0,1:T(8,128)(2,1)S(1)}, u32[]{:S(2)}, u32[]{:S(2)}) collective-permute-start(bf16[2,288]{0,1:T(8,128)(2,1)S(1)} %get-tuple-element.15), channel_id=1, source_target_pairs={{0,4},{4,8},{8,12},{12,16},{16,20},{20,24},{24,28},{1,5},{5,9},{9,... | collective-permute-start | bytes 3464 | tf_op jit(solution)/shard_map/ppermute | solution.py:14
  82.5 1.6 fusion.33
  84.1 1.6 fusion.23
  85.7 1.6 fusion.1
  87.4 2.4 %fusion.2 = bf16[256,1024]{1,0:T(8,128)(2,1)} fusion(f32[256,1024]{1,0:T(8,128)S(1)} %fusion.23, f32[256,1024]{1,0:T(8,128)S(1)} %fusion.1, bf16[5,288,1024]{2,1,0:T(8,128)(2,1)} %param.4, bf16[2,288]{0,1:T(8,128)(2,1)S(1)} %collective-permute-done.3, bf16[256,288]{0,1:T(8,128)(2,1)S(1)} %get-tuple-element.12), kind=kOutput, calls=%fused_computation.9 | convolution fusion | flops 152076288 | bytes 3359872 | tf_op jit(solution)/shard_map/dot_general | solution.py:70
  89.9 1.1 fusion.4
  90.9 1.0 fusion.6
  92.6 0.3 fusion.12
  93.0 1.6 copy-done.2
  94.6 4.6 %copy.17 = bf16[1024,1440]{1,0:T(8,128)(2,1)} copy(bf16[1024,1440]{0,1:T(8,128)(2,1)} %bitcast.63) | data formatting | bytes 5898240
  99.7 0.5 reduce_sum.57
  100.2 10.6 %reduce-scatter.5.cloned.1.call-done = bf16[256,256]{1,0:T(8,128)(2,1)} async-done(((bf16[256,1024]{1,0:T(8,128)(2,1)}), bf16[256,256]{1,0:T(8,128)(2,1)}) %reduce-scatter.5.cloned.1.call-update) | async-done | bytes 131088 | tf_op jit(solution)/shard_map/reduce_scatter | solution.py:71
  110.7 3.3 %all-to-all-start = ((bf16[4,64,256]{2,1,0:T(8,128)(2,1)}), bf16[4,64,256]{2,1,0:T(8,128)(2,1)S(1)}, u32[]{:S(2)}, u32[]{:S(2)}) async-start(bf16[4,64,256]{2,1,0:T(8,128)(2,1)} %bitcast.66), calls=%async_computation.1 | async-start | bytes 262144 | tf_op jit(solution)/shard_map/all_to_all | solution.py:74
  114.1 0.7 copy.14
  114.8 4.0 %all-to-all-done = bf16[4,64,256]{2,1,0:T(8,128)(2,1)S(1)} async-done(((bf16[4,64,256]{2,1,0:T(8,128)(2,1)}), bf16[4,64,256]{2,1,0:T(8,128)(2,1)S(1)}, u32[]{:S(2)}, u32[]{:S(2)}) %all-to-all-start) | async-done | bytes 131104 | tf_op jit(solution)/shard_map/all_to_all | solution.py:74
  119.1 0.4 mul.194
  119.4 0.4 fusion.77
  119.9 1.0 fusion.75
  120.8 39.6 %reduce-scatter.7.cloned.1.call-done = bf16[128,1440]{1,0:T(8,128)(2,1)} async-done(((bf16[1024,1440]{1,0:T(8,128)(2,1)}), bf16[128,1440]{1,0:T(8,128)(2,1)}) %reduce-scatter.7.cloned.1.call-update) | async-done | bytes 368656
  160.4 1.2 copy.18
  161.6 0.9 convert_element_type.48
  (34 shorter events, 1.6 us)
Async XLA Ops:
  7.2 30.9 %copy-start.1 = (bf16[5,288,1024]{2,1,0:T(8,128)(2,1)S(1)}, bf16[5,288,1024]{2,1,0:T(8,128)(2,1)}, u32[]{:S(2)}) copy-start(bf16[5,288,1024]{2,1,0:T(8,128)(2,1)} %param.4) | copy-start | bytes 8847364
  7.2 31.9 %copy-start.5 = (bf16[128,288]{0,1:T(8,128)(2,1)S(1)}, bf16[128,288]{0,1:T(8,128)(2,1)}, u32[]{:S(2)}) copy-start(bf16[128,288]{0,1:T(8,128)(2,1)} %param.5) | copy-start | bytes 221188
  7.2 103.6 %reduce-scatter.5.cloned.1.call-start = ((), (), s32[]{:S(2)}) async-start(), calls=%async_computation.3 | async-start | bytes 655360 | tf_op jit(solution)/shard_map/reduce_scatter | solution.py:71
  31.0 17.5 %collective-permute-start = (bf16[2,1024]{1,0:T(2,128)(2,1)}, bf16[2,1024]{1,0:T(2,128)(2,1)}, u32[]{:S(2)}, u32[]{:S(2)}) collective-permute-start(bf16[2,1024]{1,0:T(2,128)(2,1)} %get-tuple-element.10), channel_id=1, source_target_pairs={{0,4},{4,8},{8,12},{12,16},{16,20},{20,24},{24,28},{1,5},{5,9},{9,... | collective-permute-start | bytes 12296 | tf_op jit(solution)/shard_map/ppermute | solution.py:14
  36.1 10.2 %collective-permute-start.1 = (bf16[2,1024]{1,0:T(2,128)(2,1)}, bf16[2,1024]{1,0:T(2,128)(2,1)S(1)}, u32[]{:S(2)}, u32[]{:S(2)}) collective-permute-start(bf16[2,1024]{1,0:T(2,128)(2,1)} %get-tuple-element.11), channel_id=1, source_target_pairs={{4,0},{8,4},{12,8},{16,12},{20,16},{24,20},{28,24},{5,1},{9,5},{13... | collective-permute-start | bytes 12296 | tf_op jit(solution)/shard_map/ppermute | solution.py:17
  46.4 3.2 %copy-start.6 = (f32[256,288]{0,1:T(8,128)S(1)}, f32[256,288]{0,1:T(8,128)}, u32[]{:S(2)}) copy-start(f32[256,288]{0,1:T(8,128)} %fusion.31) | copy-start | bytes 884740
  47.0 3.6 %copy-start.3 = (bf16[258,1024]{1,0:T(8,128)(2,1)S(1)}, bf16[258,1024]{1,0:T(8,128)(2,1)}, u32[]{:S(2)}) copy-start(bf16[258,1024]{1,0:T(8,128)(2,1)} %constant_dynamic-update-slice_fusion) | copy-start | bytes 1585156
  71.7 10.9 %collective-permute-start.2 = (bf16[2,288]{0,1:T(8,128)(2,1)S(1)}, bf16[2,288]{0,1:T(8,128)(2,1)S(1)}, u32[]{:S(2)}, u32[]{:S(2)}) collective-permute-start(bf16[2,288]{0,1:T(8,128)(2,1)S(1)} %get-tuple-element.14), channel_id=1, source_target_pairs={{4,0},{8,4},{12,8},{16,12},{20,16},{24,20},{28,24},{5,1},{9,5},{13... | collective-permute-start | bytes 3464 | tf_op jit(solution)/shard_map/ppermute | solution.py:17
  77.1 7.0 %collective-permute-start.3 = (bf16[2,288]{0,1:T(8,128)(2,1)S(1)}, bf16[2,288]{0,1:T(8,128)(2,1)S(1)}, u32[]{:S(2)}, u32[]{:S(2)}) collective-permute-start(bf16[2,288]{0,1:T(8,128)(2,1)S(1)} %get-tuple-element.15), channel_id=1, source_target_pairs={{0,4},{4,8},{8,12},{12,16},{16,20},{20,24},{24,28},{1,5},{5,9},{9,... | collective-permute-start | bytes 3464 | tf_op jit(solution)/shard_map/ppermute | solution.py:14
  89.8 2.5 %copy-start.4 = (bf16[258,1024]{1,0:T(8,128)(2,1)S(1)}, bf16[258,1024]{1,0:T(8,128)(2,1)}, u32[]{:S(2)}) copy-start(bf16[258,1024]{1,0:T(8,128)(2,1)} %constant_dynamic-update-slice_fusion) | copy-start | bytes 1585156
  89.8 70.6 %reduce-scatter.7.cloned.1.call-start = ((), (), s32[]{:S(2)}) async-start(), calls=%async_computation.4 | async-start | bytes 3538944
  93.0 1.6 copy-start.2
  99.3 20.2 %copy-start = (bf16[128,1024]{1,0:T(8,128)(2,1)S(1)}, bf16[128,1024]{1,0:T(8,128)(2,1)}, u32[]{:S(2)}) copy-start(bf16[128,1024]{1,0:T(8,128)(2,1)} %param.3) | copy-start | bytes 786436
  110.7 8.1 %all-to-all-start = ((bf16[4,64,256]{2,1,0:T(8,128)(2,1)}), bf16[4,64,256]{2,1,0:T(8,128)(2,1)S(1)}, u32[]{:S(2)}, u32[]{:S(2)}) async-start(bf16[4,64,256]{2,1,0:T(8,128)(2,1)} %bitcast.66), calls=%async_computation.1 | async-start | bytes 262144 | tf_op jit(solution)/shard_map/all_to_all | solution.py:74
Sparse Core Ops, SparseCore 0:
  89.9 20.7 reduce-scatter.4
  114.1 46.2 reduce-scatter.6
where the time goes:
time: 171 us; the launch traced here: 169 us
  waiting for transfers between devices  54.2 us (32%)
  blocking collectives  32.3 us (19%)
  starting transfers between devices  19.7 us (12%)
  local copies, waits for them, and re-layouts  18.1 us (11%)
  matrix products  17.5 us (10%)
  between operations  14.3 us (8%)
  other arithmetic  13.1 us (8%)
    unnamed x3, waiting for transfers between devices  39.6 us
    all_gather x1, blocking collectives, per_device(): gathered = lax.all_gather(pooled, 'sub', axis=0, tiled=True)  15.3 us
    reduce_scatter x1, waiting for transfers between devices, per_device(): lax.psum_scatter(running.astype(jnp.bfloat16), 'sub', scatter_dimension=1...  10.6 us
    ppermute x2, starting transfers between devices, padded_2(): lax.ppermute(lax.slice_in_dim(block, block.shape[dim] - width, None, axis...  10.5 us
    psum x1, blocking collectives, per_device(): square_sum = lax.psum(jnp.sum(y_float * y_float, axis=1), 'sub')  10.4 us
    unnamed x19, local copies, waits for them, and re-layouts  9.81 us
    dot_general x5, matrix products, per_device(): jnp.dot(window, conv_weight[offset], preferred_element_type=jnp.float32)  8.74 us
    psum x1, blocking collectives, per_device(): lax.psum(jnp.sum(slope_second * normed_second, axis=1), 'sub')  6.63 us
  transfers between devices with their start and end apart: 7, of which 3 were waited for; matrix products, arithmetic and copies ran while one was open for 15% of the time, Pallas kernels for 0%

commit v1 on v0

--- a/solution.py
+++ b/solution.py
@@ -1,6 +1,10 @@
+import functools
+
 import jax
 import jax.numpy as jnp
 from jax import lax
+from jax.experimental import pallas as pl
+from jax.experimental.pallas import tpu as pltpu
 from jax.sharding import PartitionSpec as P
 
 EPSILON = 1e-06
@@ -31,7 +35,7 @@
     return 0.5 * jnp.sum(tensor.reshape(half_rows, 2, tensor.shape[1]), axis=1)
 
 
-def per_device(activations, conv_weight, cotangent):
+def per_device_plain(activations, conv_weight, cotangent):
     tap_count = conv_weight.shape[0]
     in_width = activations.shape[1]
     out_width = conv_weight.shape[1]
@@ -92,6 +96,363 @@
     return (features, input_grad, weight_grad)
 
 
+PAD = 16
+F32 = jnp.float32
+BF16 = jnp.bfloat16
+
+
+def gelu_half(tensor):
+    return 0.5 * (1.0 + lax.erf(tensor * 0.7071067811865476))
+
+
+def bell(tensor):
+    return tensor * jnp.exp(-0.5 * tensor * tensor) * 0.3989422804014327
+
+
+def fits(activations, conv_weight, n_seq, n_sub):
+    rows, in_width = activations.shape
+    group = rows * n_sub // 4
+    return (
+        n_seq % 2 == 0
+        and in_width % (n_seq * 128) == 0
+        and rows % 64 == 0
+        and group % 128 == 0
+        and conv_weight.shape[0] == 5
+        and conv_weight.shape[1] % 16 == 0
+        and n_seq * group <= 2048
+    )
+
+
+def kernel(
+    n_seq, n_sub,
+    x_ref, w_hbm, cot_ref,
+    feat_ref, ig_ref, wg_hbm,
+    w_ref, xs, n1, s1, p_ref, pa, gw, ga, sums, q_ref, r_ref, acc,
+    w_sem, z_send, z_recv, h_send, h_recv, a_send, a_recv, a_loc, e_send, e_recv,
+    g_send, g_recv, b_send, b_recv, l_send, l_recv, q_send, q_recv, wg_sem,
+):
+    me = lax.axis_index("sub")
+    s = lax.axis_index("seq")
+    rows, in_width = x_ref.shape
+    own = rows // 4
+    group = own * n_sub
+    ow = w_ref.shape[1]
+    full = ow * n_sub
+    cs = in_width // n_seq
+    n_chip = n_seq // 2
+    chip, core = s // 2, s % 2
+    taps = w_ref.shape[0]
+
+    def sub_id(d):
+        return lax.rem(me + d, n_sub)
+
+    def seq_id(d):
+        return lax.rem(s + d, n_seq)
+
+    def copy(src, dst, send, recv, **where):
+        return pltpu.make_async_remote_copy(
+            src_ref=src, dst_ref=dst, send_sem=send, recv_sem=recv,
+            device_id=where, device_id_type=pl.DeviceIdType.MESH,
+        )
+
+    w_copy = pltpu.make_async_copy(w_hbm, w_ref, w_sem)
+    w_copy.start()
+
+    barrier = pltpu.get_barrier_semaphore()
+    for d in range(1, n_sub):
+        pl.semaphore_signal(barrier, inc=1, device_id={"sub": sub_id(d)}, device_id_type=pl.DeviceIdType.MESH)
+    for d in range(1, n_seq):
+        pl.semaphore_signal(barrier, inc=1, device_id={"seq": seq_id(d)}, device_id_type=pl.DeviceIdType.MESH)
+
+    lanes = 128
+    for c in range(in_width // lanes):
+        xs[c] = x_ref[:, c * lanes : (c + 1) * lanes].astype(F32)
+    x_rows = [
+        jnp.concatenate([xs[c, pl.ds(r, own, stride=4), :] for c in range(in_width // lanes)], axis=1)
+        for r in range(4)
+    ]
+    inv1 = [lax.rsqrt(jnp.mean(v * v, axis=1, keepdims=True) + EPSILON) for v in x_rows]
+    mine = pl.ds(pl.multiple_of(PAD + own * me, 16), own)
+    for parity in range(2):
+        total = None
+        for r in (2 * parity, 2 * parity + 1):
+            v = x_rows[r] * inv1[r]
+            half = gelu_half(v)
+            n1[r] = v
+            s1[r] = half + bell(v)
+            total = v * half if total is None else total + v * half
+        p_ref[parity, mine, :] = (0.5 * total).astype(BF16)
+
+    pl.semaphore_wait(barrier, n_sub + n_seq - 2)
+
+    def z_copy(d, owner):
+        part = p_ref.at[:, pl.ds(pl.multiple_of(PAD + own * owner, 16), own), :]
+        return copy(part, part, z_send.at[d], z_recv.at[d], sub=sub_id(d))
+
+    for d in range(1, n_sub):
+        z_copy(d, me).start()
+    for side in (0, PAD + n_seq * group):
+        pa[:, side : side + PAD, :] = jnp.zeros((2, PAD, cs), BF16)
+    for d in range(1, n_sub):
+        z_copy(d, sub_id(n_sub - d)).wait_recv()
+
+    def up(ref, d):
+        return copy(ref.at[:, group : group + PAD, :], ref.at[:, 0:PAD, :],
+                    h_send.at[d, 0], h_recv.at[d, 0], seq=seq_id(1))
+
+    def down(ref, d):
+        return copy(ref.at[:, PAD : 2 * PAD, :], ref.at[:, group + PAD : group + 2 * PAD, :],
+                    h_send.at[d, 1], h_recv.at[d, 1], seq=seq_id(n_seq - 1))
+
+    def mask_halo(ref):
+        low = ref[:, 0:PAD, :]
+        ref[:, 0:PAD, :] = jnp.where(s == 0, jnp.zeros_like(low), low)
+        high = ref[:, group + PAD : group + 2 * PAD, :]
+        ref[:, group + PAD : group + 2 * PAD, :] = jnp.where(s == n_seq - 1, jnp.zeros_like(high), high)
+
+    up(p_ref, 0).start()
+    down(p_ref, 0).start()
+
+    def a_part(block):
+        return pa.at[:, pl.ds(pl.multiple_of(PAD + group * block, 16), group), :]
+
+    def a_copy(d, slice_of, block):
+        columns = pl.ds(pl.multiple_of(cs * slice_of, 128), cs)
+        return copy(p_ref.at[:, PAD : PAD + group, columns], a_part(block),
+                    a_send.at[d], a_recv.at[d], seq=seq_id(d))
+
+    for d in range(1, n_seq):
+        a_copy(d, seq_id(d), s).start()
+    local = pltpu.make_async_copy(
+        p_ref.at[:, PAD : PAD + group, pl.ds(pl.multiple_of(cs * s, 128), cs)], a_part(s), a_loc)
+    local.start()
+
+    up(p_ref, 0).wait_recv()
+    down(p_ref, 0).wait_recv()
+    mask_halo(p_ref)
+    w_copy.wait()
+
+    def shifts(ref_e, ref_o):
+        out = {}
+        for name, v in (("e", ref_e), ("o", ref_o)):
+            for move in (-1, 0, 1):
+                out[name, move] = v[PAD + move : PAD + move + group]
+        return out
+
+    even_taps = (("e", -1), ("o", -1), ("e", 0), ("o", 0), ("e", 1))
+    odd_taps = (("o", -1), ("e", 0), ("o", 0), ("e", 1), ("o", 1))
+
+    win = shifts(p_ref[0], p_ref[1])
+    y = None
+    for k in range(taps):
+        lhs = jnp.concatenate([win[even_taps[k]], win[odd_taps[k]]], axis=0)
+        term = lax.dot_general(lhs, w_ref[k], (((1,), (1,)), ((), ())), preferred_element_type=F32)
+        y = term if y is None else y + term
+    y = y.astype(BF16).astype(F32)
+
+    def reduce_sub(column, turn):
+        wide = jnp.broadcast_to(column, (2 * group, 128)).T
+        sums[turn, me] = wide[0:8, :]
+
+        def e_copy(d, owner):
+            part = sums.at[turn, owner]
+            return copy(part, part, e_send.at[turn, d], e_recv.at[turn, d], sub=sub_id(d))
+
+        for d in range(1, n_sub):
+            e_copy(d, me).start()
+        for d in range(1, n_sub):
+            e_copy(d, sub_id(n_sub - d)).wait_recv()
+        total = sums[turn, 0]
+        for j in range(1, n_sub):
+            total = total + sums[turn, j]
+        for d in range(1, n_sub):
+            e_copy(d, me).wait_send()
+        return jnp.concatenate([total] * 16, axis=0).T[:, 0:1]
+
+    square = reduce_sub(jnp.sum(y * y, axis=1, keepdims=True), 0)
+    inv2 = lax.rsqrt(square / full + EPSILON)
+    v2 = y * inv2
+    half = gelu_half(v2)
+    gelu2 = v2 * half
+    feat_ref[...] = (0.5 * (gelu2[0:group] + gelu2[group:])).astype(BF16)
+    cot = 0.5 * cot_ref[...].astype(F32)
+    slope = jnp.concatenate([cot, cot], axis=0) * (half + bell(v2))
+    inner = reduce_sub(jnp.sum(slope * v2, axis=1, keepdims=True), 1)
+    grad = (inv2 * (slope - v2 * (inner / full))).astype(BF16)
+    block_s = pl.ds(pl.multiple_of(PAD + group * s, 16), group)
+    for parity in range(2):
+        part = grad[parity * group : (parity + 1) * group]
+        gw[parity, PAD : PAD + group, :] = part
+        ga[parity, block_s, :] = part
+    up(gw, 1).start()
+    down(gw, 1).start()
+
+    def g_part(block):
+        return ga.at[:, pl.ds(pl.multiple_of(PAD + group * block, 16), group), :]
+
+    def g_copy(d, block):
+        target = 2 * lax.rem(chip + d, n_chip) + core
+        return copy(g_part(block), g_part(block), g_send.at[d], g_recv.at[d], seq=target)
+
+    def b_copy(d, block):
+        return copy(g_part(block), g_part(block), b_send.at[d], b_recv.at[d], seq=2 * chip + 1 - core)
+
+    b_copy(0, s).start()
+    for d in range(1, n_chip):
+        g_copy(d, s).start()
+
+    up(gw, 1).wait_recv()
+    down(gw, 1).wait_recv()
+    mask_halo(gw)
+
+    gwin = shifts(gw[0], gw[1])
+    even_back = (("e", 1), ("o", 0), ("e", 0), ("o", -1), ("e", -1))
+    odd_back = (("o", 1), ("e", 1), ("o", 0), ("e", 0), ("o", -1))
+    lhs = [jnp.concatenate([gwin[even_back[k]], gwin[odd_back[k]]], axis=0) for k in range(taps)]
+    n_col = q_send.shape[0]
+    width = in_width // n_col
+
+    def q_copy(c, d, to, owner):
+        return copy(
+            q_ref.at[c, :, pl.ds(pl.multiple_of(own * to, 16), own), :],
+            r_ref.at[owner, c],
+            q_send.at[c, d], q_recv.at[c, d], sub=sub_id(d))
+
+    for c in range(n_col):
+        total = None
+        for k in range(taps):
+            term = jnp.dot(lhs[k], w_ref[k, :, c * width : (c + 1) * width], preferred_element_type=F32)
+            total = term if total is None else total + term
+        q_ref[c] = total.astype(BF16).reshape(2, group, width)
+        for d in range(1, n_sub):
+            q_copy(c, d, sub_id(d), me).start()
+        r_ref[me, c] = q_ref[c, :, pl.ds(pl.multiple_of(own * me, 16), own), :]
+
+    for d in range(1, n_seq):
+        a_copy(d, s, seq_id(n_seq - d)).wait_recv()
+    local.wait()
+    acc[...] = jnp.zeros_like(acc)
+
+    def weight_block(block):
+        base = pl.ds(pl.multiple_of(group * block, 16), group + 2 * PAD)
+        x_win = shifts(pa[0, base, :], pa[1, base, :])
+        left = jnp.concatenate(
+            [jnp.concatenate([x_win[even_taps[k]], x_win[odd_taps[k]]], axis=0) for k in range(taps)], axis=1)
+        rows_b = pl.ds(pl.multiple_of(PAD + group * block, 16), group)
+        right = jnp.concatenate([ga[0, rows_b, :], ga[1, rows_b, :]], axis=0)
+        acc[...] += lax.dot_general(left, right, (((0,), (0,)), ((), ())), preferred_element_type=F32)
+
+    weight_block(s)
+
+    def first_pass(d, carry):
+        block = 2 * lax.rem(chip + n_chip - d, n_chip) + core
+        g_copy(d, block).wait_recv()
+        b_copy(d, block).start()
+        weight_block(block)
+        return carry
+
+    def second_pass(d, carry):
+        block = 2 * lax.rem(chip + n_chip - d, n_chip) + 1 - core
+        b_copy(d, block).wait_recv()
+        weight_block(block)
+        return carry
+
+    lax.fori_loop(1, n_chip, first_pass, 0)
+    lax.fori_loop(0, n_chip, second_pass, 0)
+    wg_copy = pltpu.make_async_copy(acc, wg_hbm, wg_sem)
+    wg_copy.start()
+
+    pg = [[], []]
+    for c in range(n_col):
+        for d in range(1, n_sub):
+            q_copy(c, d, me, sub_id(n_sub - d)).wait_recv()
+        total = r_ref[0, c].astype(F32)
+        for j in range(1, n_sub):
+            total = total + r_ref[j, c].astype(F32)
+        for parity in range(2):
+            pg[parity].append(total[parity])
+    pg = [jnp.concatenate(part, axis=1) for part in pg]
+    for r in range(4):
+        v = n1[r]
+        slope1 = 0.5 * pg[r // 2] * s1[r]
+        m1 = jnp.mean(slope1 * v, axis=1, keepdims=True)
+        out = inv1[r] * (slope1 - v * m1)
+        for c in range(in_width // lanes):
+            xs[c, pl.ds(r, own, stride=4), :] = out[:, c * lanes : (c + 1) * lanes]
+    for c in range(in_width // lanes):
+        ig_ref[:, c * lanes : (c + 1) * lanes] = xs[c].astype(BF16)
+
+    for d in range(1, n_sub):
+        z_copy(d, me).wait_send()
+        for c in range(n_col):
+            q_copy(c, d, sub_id(d), me).wait_send()
+    for d, ref in ((0, p_ref), (1, gw)):
+        up(ref, d).wait_send()
+        down(ref, d).wait_send()
+    for d in range(1, n_seq):
+        a_copy(d, seq_id(d), s).wait_send()
+    b_copy(0, s).wait_send()
+    for d in range(1, n_chip):
+        g_copy(d, s).wait_send()
+        b_copy(d, 2 * lax.rem(chip + n_chip - d, n_chip) + core).wait_send()
+    wg_copy.wait()
+
+
+def per_device(activations, conv_weight, cotangent):
+    n_seq, n_sub = lax.axis_size("seq"), lax.axis_size("sub")
+    if not fits(activations, conv_weight, n_seq, n_sub):
+        return per_device_plain(activations, conv_weight, cotangent)
+    rows, in_width = activations.shape
+    taps, ow, _ = conv_weight.shape
+    own = rows // 4
+    group = own * n_sub
+    cs = in_width // n_seq
+    n_chip = n_seq // 2
+    n_col = 4
+    width = in_width // n_col
+    dma = pltpu.SemaphoreType.DMA
+    vmem = pl.BlockSpec(memory_space=pltpu.VMEM)
+    hbm = pl.BlockSpec(memory_space=pl.ANY)
+    features, input_grad, weight_grad = pl.pallas_call(
+        functools.partial(kernel, n_seq, n_sub),
+        out_shape=(
+            jax.ShapeDtypeStruct((group, ow), BF16),
+            jax.ShapeDtypeStruct((rows, in_width), BF16),
+            jax.ShapeDtypeStruct((taps * cs, ow), F32),
+        ),
+        in_specs=[vmem, hbm, vmem],
+        out_specs=(vmem, vmem, hbm),
+        scratch_shapes=[
+            pltpu.VMEM((taps, ow, in_width), BF16),
+            pltpu.VMEM((in_width // 128, rows, 128), F32),
+            pltpu.VMEM((4, own, in_width), F32),
+            pltpu.VMEM((4, own, in_width), F32),
+            pltpu.VMEM((2, group + 2 * PAD, in_width), BF16),
+            pltpu.VMEM((2, n_seq * group + 2 * PAD, cs), BF16),
+            pltpu.VMEM((2, group + 2 * PAD, ow), BF16),
+            pltpu.VMEM((2, n_seq * group + 2 * PAD, ow), BF16),
+            pltpu.VMEM((2, n_sub, 8, 2 * group), F32),
+            pltpu.VMEM((n_col, 2, group, width), BF16),
+            pltpu.VMEM((n_sub, n_col, 2, own, width), BF16),
+            pltpu.VMEM((taps * cs, ow), F32),
+            dma, dma((n_sub,)), dma((n_sub,)), dma((2, 2)), dma((2, 2)),
+            dma((n_seq,)), dma((n_seq,)), dma, dma((2, n_sub)), dma((2, n_sub)),
+            dma((n_chip,)), dma((n_chip,)), dma((n_chip,)), dma((n_chip,)),
+            dma, dma, dma((n_col, n_sub)), dma((n_col, n_sub)), dma,
+        ],
+        compiler_params=pltpu.CompilerParams(
+            collective_id=0, has_side_effects=True, vmem_limit_bytes=44 * 1024 * 1024
+        ),
+        cost_estimate=pl.CostEstimate(
+            flops=6 * 2 * group * taps * ow * in_width,
+            bytes_accessed=2 * taps * ow * in_width,
+            transcendentals=2 * rows * in_width,
+        ),
+    )(activations, conv_weight, cotangent)
+    weight_grad = weight_grad.reshape(taps, cs, ow).transpose(1, 0, 2)
+    return (features, input_grad, weight_grad)
+
+
 def solution(mesh):
     return jax.shard_map(
         per_device,

time: 171 us -> 55.3 us (0.32)
  the two profiles are of different devices: /device:TPU:1 before, /device:TPU:0 now
where the time goes in v1:
time: 55.3 us; the launch traced here: 55.1 us
  Pallas kernels  48.1 us (87%)
  local copies, waits for them, and re-layouts  6.4 us (12%)
  between operations  0.65 us (1%)
    pallas_call x1, Pallas kernels, per_device(): pl.pallas_call(functools.partial(kernel, n_seq, n_sub), out_shape=(jax.Sh...  48.1 us
    unnamed x7, local copies, waits for them, and re-layouts  5.22 us
    reshape x1, local copies, waits for them, and re-layouts, per_device(): weight_grad = weight_grad.reshape(taps, cs, ow).transpose(1, 0, 2)  1.17 us

profile of v1, /device:TPU:0, one launch (start us, length us, event | category | flops | bytes accessed | tf_op | source)
XLA Modules:
  0.0 55.1 jit_solution(13524290209431179420)
XLA Ops:
  0.6 1.0 %copy.6.cot_ref = bf16[128,288]{1,0:T(8,128)(2,1)S(1)} copy(bf16[128,288]{0,1:T(8,128)(2,1)} %param.5) | data formatting | bytes 147456 | tf_op args[2]
  1.6 0.0 copy-start
  1.6 1.8 %copy-done = bf16[5,288,1024]{2,1,0:T(8,128)(2,1)S(1)} copy-done((bf16[5,288,1024]{2,1,0:T(8,128)(2,1)S(1)}, bf16[5,288,1024]{2,1,0:T(8,128)(2,1)}, u32[]{:S(2)}) %copy-start) | copy-done | bytes 2949144
  3.5 0.0 copy-start.1
  3.5 0.9 %copy-done.1 = bf16[128,1024]{1,0:T(8,128)(2,1)S(1)} copy-done((bf16[128,1024]{1,0:T(8,128)(2,1)S(1)}, bf16[128,1024]{1,0:T(8,128)(2,1)}, u32[]{:S(2)}) %copy-start.1) | copy-done | bytes 262168
  4.4 48.1 %shard_map.58 = (bf16[128,288]{1,0:T(8,128)(2,1)S(1)}, bf16[128,1024]{1,0:T(8,128)(2,1)S(1)}, f32[640,288]{1,0:T(8,128)S(1)}) custom-call(bf16[128,1024]{1,0:T(8,128)(2,1)S(1)} %copy-done.1, bf16[5,288,1024]{2,1,0:T(8,128)(2,1)S(1)} %copy-done, bf16[128,288]{1,0:T(8,128)(2,1)S(1)} %copy.6.cot_ref), custom_call_target="tpu_custom_call" | custom-call | flops 2264924160 | bytes 2949120 | tf_op jit(solution)/shard_map/pallas_call | solution.py:416
  52.5 0.7 %copy.8 = bf16[128,288]{0,1:T(8,128)(2,1)} copy(bf16[128,288]{1,0:T(8,128)(2,1)S(1)} %get-tuple-element.9) | data formatting | bytes 147456
  53.2 1.2 %copy.7 = f32[5,128,288]{1,2,0:T(8,128)} copy(f32[5,128,288]{2,1,0:T(8,128)S(1)} %bitcast.2) | data formatting | bytes 1474560 | tf_op jit(solution)/shard_map/reshape | solution.py:452
  54.4 0.7 %copy.10 = bf16[128,1024]{1,0:T(8,128)(2,1)} copy(bf16[128,1024]{1,0:T(8,128)(2,1)S(1)} %get-tuple-element.16) | data formatting | bytes 524288
Async XLA Ops:
  1.6 1.8 %copy-start = (bf16[5,288,1024]{2,1,0:T(8,128)(2,1)S(1)}, bf16[5,288,1024]{2,1,0:T(8,128)(2,1)}, u32[]{:S(2)}) copy-start(bf16[5,288,1024]{2,1,0:T(8,128)(2,1)} %w_hbm.1) | copy-start | bytes 8847364
  3.5 0.9 %copy-start.1 = (bf16[128,1024]{1,0:T(8,128)(2,1)S(1)}, bf16[128,1024]{1,0:T(8,128)(2,1)}, u32[]{:S(2)}) copy-start(bf16[128,1024]{1,0:T(8,128)(2,1)} %x_ref.1) | copy-start | bytes 786436

commit v2 on v1

--- a/solution.py
+++ b/solution.py
@@ -97,6 +97,7 @@
 
 
 PAD = 16
+VMEM_BYTES = 60 * 1024 * 1024
 F32 = jnp.float32
 BF16 = jnp.bfloat16
 
@@ -124,24 +125,25 @@
 
 
 def kernel(
-    n_seq, n_sub,
-    x_ref, w_hbm, cot_ref,
-    feat_ref, ig_ref, wg_hbm,
-    w_ref, xs, n1, s1, p_ref, pa, gw, ga, sums, q_ref, r_ref, acc,
-    w_sem, z_send, z_recv, h_send, h_recv, a_send, a_recv, a_loc, e_send, e_recv,
-    g_send, g_recv, b_send, b_recv, l_send, l_recv, q_send, q_recv, wg_sem,
+    n_seq, n_sub, taps,
+    x_hbm, w_hbm, cot_hbm,
+    feat_hbm, ig_hbm, wg_hbm,
+    x_ref, w_ref, cot_ref, feat_ref, ig_ref, xs, n1, s1, p_ref, pa, gw, ga, sums, q_ref, r_ref, acc,
+    in_sem, out_sem, z_send, z_recv, h_send, h_recv, k_send, k_recv, a_send, a_recv, a_loc, e_send, e_recv,
+    g_send, g_recv, b_send, b_recv, q_send, q_recv,
 ):
     me = lax.axis_index("sub")
     s = lax.axis_index("seq")
     rows, in_width = x_ref.shape
     own = rows // 4
     group = own * n_sub
-    ow = w_ref.shape[1]
+    ow = w_ref.shape[0] // taps
     full = ow * n_sub
     cs = in_width // n_seq
     n_chip = n_seq // 2
     chip, core = s // 2, s % 2
-    taps = w_ref.shape[0]
+    n_col = q_send.shape[0]
+    width = in_width // n_col
 
     def sub_id(d):
         return lax.rem(me + d, n_sub)
@@ -155,20 +157,28 @@
             device_id=where, device_id_type=pl.DeviceIdType.MESH,
         )
 
-    w_copy = pltpu.make_async_copy(w_hbm, w_ref, w_sem)
-    w_copy.start()
+    loads = [
+        pltpu.make_async_copy(src, dst, in_sem.at[i])
+        for i, (src, dst) in enumerate(((x_hbm, x_ref), (w_hbm, w_ref), (cot_hbm, cot_ref)))
+    ]
+    for load in loads:
+        load.start()
 
     barrier = pltpu.get_barrier_semaphore()
     for d in range(1, n_sub):
         pl.semaphore_signal(barrier, inc=1, device_id={"sub": sub_id(d)}, device_id_type=pl.DeviceIdType.MESH)
     for d in range(1, n_seq):
         pl.semaphore_signal(barrier, inc=1, device_id={"seq": seq_id(d)}, device_id_type=pl.DeviceIdType.MESH)
+    for side in (0, PAD + n_seq * group):
+        pa[:, side : side + PAD, :] = jnp.zeros((2, PAD, cs), BF16)
+    loads[0].wait()
 
     lanes = 128
-    for c in range(in_width // lanes):
+    n_lane = in_width // lanes
+    for c in range(n_lane):
         xs[c] = x_ref[:, c * lanes : (c + 1) * lanes].astype(F32)
     x_rows = [
-        jnp.concatenate([xs[c, pl.ds(r, own, stride=4), :] for c in range(in_width // lanes)], axis=1)
+        jnp.concatenate([xs[c, pl.ds(r, own, stride=4), :] for c in range(n_lane)], axis=1)
         for r in range(4)
     ]
     inv1 = [lax.rsqrt(jnp.mean(v * v, axis=1, keepdims=True) + EPSILON) for v in x_rows]
@@ -179,39 +189,78 @@
             v = x_rows[r] * inv1[r]
             half = gelu_half(v)
             n1[r] = v
-            s1[r] = half + bell(v)
+            s1[r] = half
             total = v * half if total is None else total + v * half
         p_ref[parity, mine, :] = (0.5 * total).astype(BF16)
 
     pl.semaphore_wait(barrier, n_sub + n_seq - 2)
 
-    def z_copy(d, owner):
-        part = p_ref.at[:, pl.ds(pl.multiple_of(PAD + own * owner, 16), own), :]
-        return copy(part, part, z_send.at[d], z_recv.at[d], sub=sub_id(d))
-
-    for d in range(1, n_sub):
-        z_copy(d, me).start()
-    for side in (0, PAD + n_seq * group):
-        pa[:, side : side + PAD, :] = jnp.zeros((2, PAD, cs), BF16)
-    for d in range(1, n_sub):
-        z_copy(d, sub_id(n_sub - d)).wait_recv()
-
-    def up(ref, d):
-        return copy(ref.at[:, group : group + PAD, :], ref.at[:, 0:PAD, :],
-                    h_send.at[d, 0], h_recv.at[d, 0], seq=seq_id(1))
-
-    def down(ref, d):
+    def cols(c):
+        return slice(c * width, (c + 1) * width)
+
+    def z_copy(c, d, owner):
+        part = p_ref.at[:, pl.ds(pl.multiple_of(PAD + own * owner, 16), own), cols(c)]
+        return copy(part, part, z_send.at[c, d], z_recv.at[c, d], sub=sub_id(d))
+
+    for c in range(n_col):
+        for d in range(1, n_sub):
+            z_copy(c, d, me).start()
+    for r in range(4):
+        s1[r] += bell(n1[r])
+
+    def up(ref, send, recv):
+        return copy(ref.at[:, group : group + PAD, :], ref.at[:, 0:PAD, :], send, recv, seq=seq_id(1))
+
+    def down(ref, send, recv):
         return copy(ref.at[:, PAD : 2 * PAD, :], ref.at[:, group + PAD : group + 2 * PAD, :],
-                    h_send.at[d, 1], h_recv.at[d, 1], seq=seq_id(n_seq - 1))
-
-    def mask_halo(ref):
-        low = ref[:, 0:PAD, :]
-        ref[:, 0:PAD, :] = jnp.where(s == 0, jnp.zeros_like(low), low)
-        high = ref[:, group + PAD : group + 2 * PAD, :]
-        ref[:, group + PAD : group + 2 * PAD, :] = jnp.where(s == n_seq - 1, jnp.zeros_like(high), high)
-
-    up(p_ref, 0).start()
-    down(p_ref, 0).start()
+                    send, recv, seq=seq_id(n_seq - 1))
+
+    def halo_pooled(c):
+        part = p_ref.at[:, :, cols(c)]
+        return (up(part, h_send.at[c, 0], h_recv.at[c, 0]), down(part, h_send.at[c, 1], h_recv.at[c, 1]))
+
+    def halo_grad():
+        return (up(gw, k_send.at[0], k_recv.at[0]), down(gw, k_send.at[1], k_recv.at[1]))
+
+    def shifts(v_e, v_o):
+        return {
+            (name, move): v[PAD + move : PAD + move + group]
+            for name, v in (("e", v_e), ("o", v_o))
+            for move in (-1, 0, 1)
+        }
+
+    def edges(v):
+        low, middle, high = v[:, 0:PAD], v[:, PAD : PAD + group], v[:, PAD + group :]
+        low = jnp.where(s == 0, jnp.zeros_like(low), low)
+        high = jnp.where(s == n_seq - 1, jnp.zeros_like(high), high)
+        return jnp.concatenate([low, middle, high], axis=1)
+
+    even_taps = (("e", -1), ("o", -1), ("e", 0), ("o", 0), ("e", 1))
+    odd_taps = (("o", -1), ("e", 0), ("o", 0), ("e", 1), ("o", 1))
+
+    def tap_windows(win):
+        return jnp.concatenate(
+            [jnp.concatenate([win[even_taps[k]], win[odd_taps[k]]], axis=0) for k in range(taps)], axis=1)
+
+    def conv_block(c):
+        for halo in halo_pooled(c):
+            halo.wait_recv()
+        v = edges(p_ref[:, :, cols(c)])
+        right = tap_windows(shifts(v[0], v[1]))
+        left = jnp.concatenate([w_ref[k * ow : (k + 1) * ow, cols(c)] for k in range(taps)], axis=1)
+        return lax.dot_general(left, right, (((1,), (1,)), ((), ())), preferred_element_type=F32)
+
+    y = None
+    for c in range(n_col):
+        for d in range(1, n_sub):
+            z_copy(c, d, sub_id(n_sub - d)).wait_recv()
+        for halo in halo_pooled(c):
+            halo.start()
+        if c == 0:
+            loads[1].wait()
+        else:
+            term = conv_block(c - 1)
+            y = term if y is None else y + term
 
     def a_part(block):
         return pa.at[:, pl.ds(pl.multiple_of(PAD + group * block, 16), group), :]
@@ -226,91 +275,69 @@
     local = pltpu.make_async_copy(
         p_ref.at[:, PAD : PAD + group, pl.ds(pl.multiple_of(cs * s, 128), cs)], a_part(s), a_loc)
     local.start()
-
-    up(p_ref, 0).wait_recv()
-    down(p_ref, 0).wait_recv()
-    mask_halo(p_ref)
-    w_copy.wait()
-
-    def shifts(ref_e, ref_o):
-        out = {}
-        for name, v in (("e", ref_e), ("o", ref_o)):
-            for move in (-1, 0, 1):
-                out[name, move] = v[PAD + move : PAD + move + group]
-        return out
-
-    even_taps = (("e", -1), ("o", -1), ("e", 0), ("o", 0), ("e", 1))
-    odd_taps = (("o", -1), ("e", 0), ("o", 0), ("e", 1), ("o", 1))
-
-    win = shifts(p_ref[0], p_ref[1])
-    y = None
-    for k in range(taps):
-        lhs = jnp.concatenate([win[even_taps[k]], win[odd_taps[k]]], axis=0)
-        term = lax.dot_general(lhs, w_ref[k], (((1,), (1,)), ((), ())), preferred_element_type=F32)
-        y = term if y is None else y + term
+    y = y + conv_block(n_col - 1)
     y = y.astype(BF16).astype(F32)
 
-    def reduce_sub(column, turn):
-        wide = jnp.broadcast_to(column, (2 * group, 128)).T
-        sums[turn, me] = wide[0:8, :]
-
-        def e_copy(d, owner):
-            part = sums.at[turn, owner]
-            return copy(part, part, e_send.at[turn, d], e_recv.at[turn, d], sub=sub_id(d))
-
-        for d in range(1, n_sub):
-            e_copy(d, me).start()
-        for d in range(1, n_sub):
-            e_copy(d, sub_id(n_sub - d)).wait_recv()
+    def e_copy(turn, d, owner):
+        part = sums.at[turn, owner]
+        return copy(part, part, e_send.at[turn, d], e_recv.at[turn, d], sub=sub_id(d))
+
+    def reduce_start(turn, values):
+        sums[turn, me] = jnp.broadcast_to(jnp.sum(values, axis=0, keepdims=True), (8, 2 * group))
+        for d in range(1, n_sub):
+            e_copy(turn, d, me).start()
+
+    def reduce_end(turn):
+        for d in range(1, n_sub):
+            e_copy(turn, d, sub_id(n_sub - d)).wait_recv()
         total = sums[turn, 0]
         for j in range(1, n_sub):
             total = total + sums[turn, j]
-        for d in range(1, n_sub):
-            e_copy(d, me).wait_send()
-        return jnp.concatenate([total] * 16, axis=0).T[:, 0:1]
-
-    square = reduce_sub(jnp.sum(y * y, axis=1, keepdims=True), 0)
-    inv2 = lax.rsqrt(square / full + EPSILON)
+        return total[0:1, :]
+
+    reduce_start(0, y * y)
+    loads[2].wait()
+    cot = 0.5 * cot_ref[...].astype(F32)
+    inv2 = lax.rsqrt(reduce_end(0) / full + EPSILON)
     v2 = y * inv2
     half = gelu_half(v2)
+    slope = jnp.concatenate([cot, cot], axis=1) * (half + bell(v2))
+    reduce_start(1, slope * v2)
     gelu2 = v2 * half
-    feat_ref[...] = (0.5 * (gelu2[0:group] + gelu2[group:])).astype(BF16)
-    cot = 0.5 * cot_ref[...].astype(F32)
-    slope = jnp.concatenate([cot, cot], axis=0) * (half + bell(v2))
-    inner = reduce_sub(jnp.sum(slope * v2, axis=1, keepdims=True), 1)
-    grad = (inv2 * (slope - v2 * (inner / full))).astype(BF16)
-    block_s = pl.ds(pl.multiple_of(PAD + group * s, 16), group)
+    feat_ref[...] = (0.5 * (gelu2[:, 0:group] + gelu2[:, group:])).astype(BF16)
+    outs = [
+        pltpu.make_async_copy(src, dst, out_sem.at[i])
+        for i, (src, dst) in enumerate(((feat_ref, feat_hbm), (ig_ref, ig_hbm), (acc, wg_hbm)))
+    ]
+    outs[0].start()
+    inner = reduce_end(1)
+    grad = inv2 * (slope - v2 * (inner / full))
+    turned = grad.T.astype(BF16)
     for parity in range(2):
-        part = grad[parity * group : (parity + 1) * group]
-        gw[parity, PAD : PAD + group, :] = part
-        ga[parity, block_s, :] = part
-    up(gw, 1).start()
-    down(gw, 1).start()
-
-    def g_part(block):
-        return ga.at[:, pl.ds(pl.multiple_of(PAD + group * block, 16), group), :]
+        gw[parity, PAD : PAD + group, :] = turned[parity * group : (parity + 1) * group]
+    for halo in halo_grad():
+        halo.start()
+    ga[s] = grad.astype(BF16)
 
     def g_copy(d, block):
         target = 2 * lax.rem(chip + d, n_chip) + core
-        return copy(g_part(block), g_part(block), g_send.at[d], g_recv.at[d], seq=target)
+        return copy(ga.at[block], ga.at[block], g_send.at[d], g_recv.at[d], seq=target)
 
     def b_copy(d, block):
-        return copy(g_part(block), g_part(block), b_send.at[d], b_recv.at[d], seq=2 * chip + 1 - core)
+        return copy(ga.at[block], ga.at[block], b_send.at[d], b_recv.at[d], seq=2 * chip + 1 - core)
 
     b_copy(0, s).start()
     for d in range(1, n_chip):
         g_copy(d, s).start()
 
-    up(gw, 1).wait_recv()
-    down(gw, 1).wait_recv()
-    mask_halo(gw)
-
-    gwin = shifts(gw[0], gw[1])
+    for halo in halo_grad():
+        halo.wait_recv()
+    v = edges(gw[...])
+    win = shifts(v[0], v[1])
     even_back = (("e", 1), ("o", 0), ("e", 0), ("o", -1), ("e", -1))
     odd_back = (("o", 1), ("e", 1), ("o", 0), ("e", 0), ("o", -1))
-    lhs = [jnp.concatenate([gwin[even_back[k]], gwin[odd_back[k]]], axis=0) for k in range(taps)]
-    n_col = q_send.shape[0]
-    width = in_width // n_col
+    left = jnp.concatenate(
+        [jnp.concatenate([win[even_back[k]], win[odd_back[k]]], axis=0) for k in range(taps)], axis=1)
 
     def q_copy(c, d, to, owner):
         return copy(
@@ -319,10 +346,7 @@
             q_send.at[c, d], q_recv.at[c, d], sub=sub_id(d))
 
     for c in range(n_col):
-        total = None
-        for k in range(taps):
-            term = jnp.dot(lhs[k], w_ref[k, :, c * width : (c + 1) * width], preferred_element_type=F32)
-            total = term if total is None else total + term
+        total = jnp.dot(left, w_ref[:, cols(c)], preferred_element_type=F32)
         q_ref[c] = total.astype(BF16).reshape(2, group, width)
         for d in range(1, n_sub):
             q_copy(c, d, sub_id(d), me).start()
@@ -335,12 +359,10 @@
 
     def weight_block(block):
         base = pl.ds(pl.multiple_of(group * block, 16), group + 2 * PAD)
-        x_win = shifts(pa[0, base, :], pa[1, base, :])
-        left = jnp.concatenate(
-            [jnp.concatenate([x_win[even_taps[k]], x_win[odd_taps[k]]], axis=0) for k in range(taps)], axis=1)
-        rows_b = pl.ds(pl.multiple_of(PAD + group * block, 16), group)
-        right = jnp.concatenate([ga[0, rows_b, :], ga[1, rows_b, :]], axis=0)
-        acc[...] += lax.dot_general(left, right, (((0,), (0,)), ((), ())), preferred_element_type=F32)
+        right = tap_windows(shifts(pa[0, base, :], pa[1, base, :]))
+        term = jnp.dot(ga[block], right, preferred_element_type=F32)
+        for k in range(taps):
+            acc[k] += term[:, k * cs : (k + 1) * cs]
 
     weight_block(s)
 
@@ -359,8 +381,7 @@
 
     lax.fori_loop(1, n_chip, first_pass, 0)
     lax.fori_loop(0, n_chip, second_pass, 0)
-    wg_copy = pltpu.make_async_copy(acc, wg_hbm, wg_sem)
-    wg_copy.start()
+    outs[2].start()
 
     pg = [[], []]
     for c in range(n_col):
@@ -377,25 +398,31 @@
         slope1 = 0.5 * pg[r // 2] * s1[r]
         m1 = jnp.mean(slope1 * v, axis=1, keepdims=True)
         out = inv1[r] * (slope1 - v * m1)
-        for c in range(in_width // lanes):
+        for c in range(n_lane):
             xs[c, pl.ds(r, own, stride=4), :] = out[:, c * lanes : (c + 1) * lanes]
-    for c in range(in_width // lanes):
+    for c in range(n_lane):
         ig_ref[:, c * lanes : (c + 1) * lanes] = xs[c].astype(BF16)
+    outs[1].start()
 
     for d in range(1, n_sub):
-        z_copy(d, me).wait_send()
         for c in range(n_col):
+            z_copy(c, d, me).wait_send()
             q_copy(c, d, sub_id(d), me).wait_send()
-    for d, ref in ((0, p_ref), (1, gw)):
-        up(ref, d).wait_send()
-        down(ref, d).wait_send()
+        for turn in range(2):
+            e_copy(turn, d, me).wait_send()
+    for c in range(n_col):
+        for halo in halo_pooled(c):
+            halo.wait_send()
+    for halo in halo_grad():
+        halo.wait_send()
     for d in range(1, n_seq):
         a_copy(d, seq_id(d), s).wait_send()
     b_copy(0, s).wait_send()
     for d in range(1, n_chip):
         g_copy(d, s).wait_send()
         b_copy(d, 2 * lax.rem(chip + n_chip - d, n_chip) + core).wait_send()
-    wg_copy.wait()
+    for out in outs:
+        out.wait()
 
 
 def per_device(activations, conv_weight, cotangent):
@@ -411,46 +438,49 @@
     n_col = 4
     width = in_width // n_col
     dma = pltpu.SemaphoreType.DMA
-    vmem = pl.BlockSpec(memory_space=pltpu.VMEM)
     hbm = pl.BlockSpec(memory_space=pl.ANY)
     features, input_grad, weight_grad = pl.pallas_call(
-        functools.partial(kernel, n_seq, n_sub),
+        functools.partial(kernel, n_seq, n_sub, taps),
         out_shape=(
-            jax.ShapeDtypeStruct((group, ow), BF16),
+            jax.ShapeDtypeStruct((ow, group), BF16),
             jax.ShapeDtypeStruct((rows, in_width), BF16),
-            jax.ShapeDtypeStruct((taps * cs, ow), F32),
+            jax.ShapeDtypeStruct((taps, ow, cs), F32),
         ),
-        in_specs=[vmem, hbm, vmem],
-        out_specs=(vmem, vmem, hbm),
+        in_specs=[hbm, hbm, hbm],
+        out_specs=(hbm, hbm, hbm),
         scratch_shapes=[
-            pltpu.VMEM((taps, ow, in_width), BF16),
+            pltpu.VMEM((rows, in_width), BF16),
+            pltpu.VMEM((taps * ow, in_width), BF16),
+            pltpu.VMEM((ow, group), BF16),
+            pltpu.VMEM((ow, group), BF16),
+            pltpu.VMEM((rows, in_width), BF16),
             pltpu.VMEM((in_width // 128, rows, 128), F32),
             pltpu.VMEM((4, own, in_width), F32),
             pltpu.VMEM((4, own, in_width), F32),
             pltpu.VMEM((2, group + 2 * PAD, in_width), BF16),
             pltpu.VMEM((2, n_seq * group + 2 * PAD, cs), BF16),
             pltpu.VMEM((2, group + 2 * PAD, ow), BF16),
-            pltpu.VMEM((2, n_seq * group + 2 * PAD, ow), BF16),
+            pltpu.VMEM((n_seq, ow, 2 * group), BF16),
             pltpu.VMEM((2, n_sub, 8, 2 * group), F32),
             pltpu.VMEM((n_col, 2, group, width), BF16),
             pltpu.VMEM((n_sub, n_col, 2, own, width), BF16),
-            pltpu.VMEM((taps * cs, ow), F32),
-            dma, dma((n_sub,)), dma((n_sub,)), dma((2, 2)), dma((2, 2)),
+            pltpu.VMEM((taps, ow, cs), F32),
+            dma((3,)), dma((3,)), dma((n_col, n_sub)), dma((n_col, n_sub)),
+            dma((n_col, 2)), dma((n_col, 2)), dma((2,)), dma((2,)),
             dma((n_seq,)), dma((n_seq,)), dma, dma((2, n_sub)), dma((2, n_sub)),
             dma((n_chip,)), dma((n_chip,)), dma((n_chip,)), dma((n_chip,)),
-            dma, dma, dma((n_col, n_sub)), dma((n_col, n_sub)), dma,
+            dma((n_col, n_sub)), dma((n_col, n_sub)),
         ],
         compiler_params=pltpu.CompilerParams(
-            collective_id=0, has_side_effects=True, vmem_limit_bytes=44 * 1024 * 1024
+            collective_id=0, has_side_effects=True, vmem_limit_bytes=VMEM_BYTES
         ),
         cost_estimate=pl.CostEstimate(
             flops=6 * 2 * group * taps * ow * in_width,
             bytes_accessed=2 * taps * ow * in_width,
             transcendentals=2 * rows * in_width,
         ),
-    )(activations, conv_weight, cotangent)
-    weight_grad = weight_grad.reshape(taps, cs, ow).transpose(1, 0, 2)
-    return (features, input_grad, weight_grad)
+    )(activations, conv_weight.reshape(taps * ow, in_width), cotangent.T)
+    return (features.T, input_grad, weight_grad.transpose(2, 0, 1))
 
 
 def solution(mesh):

time: 55.3 us -> 52.4 us (0.948)
  the two profiles are of different devices: /device:TPU:0 before, /device:TPU:1 now
where the time goes in v2:
time: 52.4 us; the launch traced here: 52.2 us
  Pallas kernels  46.3 us (88%)
  local copies, waits for them, and re-layouts  5.22 us (10%)
  between operations  0.64 us (1%)
    pallas_call x1, Pallas kernels, per_device(): pl.pallas_call(functools.partial(kernel, n_seq, n_sub, taps), out_shape=(...  46.3 us
    unnamed x3, local copies, waits for them, and re-layouts  5.22 us

profile of v2, /device:TPU:1, one launch (start us, length us, event | category | flops | bytes accessed | tf_op | source)
XLA Modules:
  0.0 52.2 jit_solution(2609137602396351403)
XLA Ops:
  0.6 46.3 %shard_map.58 = (bf16[288,128]{1,0:T(8,128)(2,1)}, bf16[128,1024]{1,0:T(8,128)(2,1)}, f32[5,288,128]{2,1,0:T(8,128)}) custom-call(bf16[128,1024]{1,0:T(8,128)(2,1)} %x_hbm.1, bf16[1440,1024]{1,0:T(8,128)(2,1)} %bitcast.6, bf16[288,128]{1,0:T(8,128)(2,1)} %bitcast.7), custom_call_target="tpu_custom_call" | custom-call | flops 2264924160 | bytes 2949120 | tf_op jit(solution)/shard_map/pallas_call | solution.py:442
  46.9 1.5 %copy.9 = bf16[128,288]{0,1:T(8,128)(2,1)} copy(bf16[128,288]{0,1:T(8,128)(2,1)} %bitcast.5) | data formatting | bytes 147456
  48.5 1.7 %copy.10 = bf16[128,1024]{1,0:T(8,128)(2,1)} copy(bf16[128,1024]{1,0:T(8,128)(2,1)} %get-tuple-element.13) | data formatting | bytes 524288
  50.1 2.0 %copy.11 = f32[128,5,288]{0,2,1:T(8,128)} copy(f32[128,5,288]{0,2,1:T(8,128)} %bitcast.4) | data formatting | bytes 1474560

commit v3 on v2

--- a/solution.py
+++ b/solution.py
@@ -198,13 +198,39 @@
     def cols(c):
         return slice(c * width, (c + 1) * width)
 
-    def z_copy(c, d, owner):
+    ways = ((1, n_sub - 1), (-1, 0))
+
+    def z_copy(c, way, t, owner):
+        step = ways[way][0]
         part = p_ref.at[:, pl.ds(pl.multiple_of(PAD + own * owner, 16), own), cols(c)]
-        return copy(part, part, z_send.at[c, d], z_recv.at[c, d], sub=sub_id(d))
+        target = lax.rem(me + step + n_sub, n_sub)
+        return copy(part, part, z_send.at[c, way, t - 1], z_recv.at[c, way, t - 1], sub=target)
+
+    def has(way, t):
+        return me >= t if way == 0 else me + t < n_sub
+
+    def z_send_all(t, c, act):
+        for way in range(2):
+            step, last = ways[way]
+            source = me - step * (t - 1)
+
+            @pl.when(jnp.logical_and(has(way, t - 1), me != last))
+            def _():
+                act(z_copy(c, way, t, source))
+
+    def z_wait(t, c):
+        for way in range(2):
+            step, last = ways[way]
+
+            @pl.when(has(way, t))
+            def _():
+                z_copy(c, way, t, me - step * t).wait_recv()
+
+    def z_start(t, c):
+        z_send_all(t, c, lambda one: one.start())
 
     for c in range(n_col):
-        for d in range(1, n_sub):
-            z_copy(c, d, me).start()
+        z_start(1, c)
     for r in range(4):
         s1[r] += bell(n1[r])
 
@@ -251,9 +277,12 @@
         return lax.dot_general(left, right, (((1,), (1,)), ((), ())), preferred_element_type=F32)
 
     y = None
+    for t in range(1, n_sub - 1):
+        for c in range(n_col):
+            z_wait(t, c)
+            z_start(t + 1, c)
     for c in range(n_col):
-        for d in range(1, n_sub):
-            z_copy(c, d, sub_id(n_sub - d)).wait_recv()
+        z_wait(n_sub - 1, c)
         for halo in halo_pooled(c):
             halo.start()
         if c == 0:
@@ -406,7 +435,7 @@
 
     for d in range(1, n_sub):
         for c in range(n_col):
-            z_copy(c, d, me).wait_send()
+            z_send_all(d, c, lambda one: one.wait_send())
             q_copy(c, d, sub_id(d), me).wait_send()
         for turn in range(2):
             e_copy(turn, d, me).wait_send()
@@ -425,6 +454,27 @@
         out.wait()
 
 
+def hand_over_kernel(*refs):
+    count = len(refs) // 2
+    sems = refs[-1]
+    moves = [pltpu.make_async_copy(refs[i], refs[count + i], sems.at[i]) for i in range(count)]
+    for move in moves:
+        move.start()
+    for move in moves:
+        move.wait()
+
+
+def hand_over(*arrays):
+    hbm = pl.BlockSpec(memory_space=pl.ANY)
+    return pl.pallas_call(
+        hand_over_kernel,
+        out_shape=tuple(jax.ShapeDtypeStruct(a.shape, a.dtype) for a in arrays),
+        in_specs=[hbm] * len(arrays),
+        out_specs=(hbm,) * len(arrays),
+        scratch_shapes=[pltpu.SemaphoreType.DMA((len(arrays),))],
+    )(*arrays)
+
+
 def per_device(activations, conv_weight, cotangent):
     n_seq, n_sub = lax.axis_size("seq"), lax.axis_size("sub")
     if not fits(activations, conv_weight, n_seq, n_sub):
@@ -439,6 +489,7 @@
     width = in_width // n_col
     dma = pltpu.SemaphoreType.DMA
     hbm = pl.BlockSpec(memory_space=pl.ANY)
+    far = pl.BlockSpec(memory_space=pltpu.HBM)
     features, input_grad, weight_grad = pl.pallas_call(
         functools.partial(kernel, n_seq, n_sub, taps),
         out_shape=(
@@ -446,7 +497,7 @@
             jax.ShapeDtypeStruct((rows, in_width), BF16),
             jax.ShapeDtypeStruct((taps, ow, cs), F32),
         ),
-        in_specs=[hbm, hbm, hbm],
+        in_specs=[far, far, far],
         out_specs=(hbm, hbm, hbm),
         scratch_shapes=[
             pltpu.VMEM((rows, in_width), BF16),
@@ -465,7 +516,7 @@
             pltpu.VMEM((n_col, 2, group, width), BF16),
             pltpu.VMEM((n_sub, n_col, 2, own, width), BF16),
             pltpu.VMEM((taps, ow, cs), F32),
-            dma((3,)), dma((3,)), dma((n_col, n_sub)), dma((n_col, n_sub)),
+            dma((3,)), dma((3,)), dma((n_col, 2, n_sub)), dma((n_col, 2, n_sub)),
             dma((n_col, 2)), dma((n_col, 2)), dma((2,)), dma((2,)),
             dma((n_seq,)), dma((n_seq,)), dma, dma((2, n_sub)), dma((2, n_sub)),
             dma((n_chip,)), dma((n_chip,)), dma((n_chip,)), dma((n_chip,)),
@@ -480,6 +531,7 @@
             transcendentals=2 * rows * in_width,
         ),
     )(activations, conv_weight.reshape(taps * ow, in_width), cotangent.T)
+    features, input_grad, weight_grad = hand_over(features, input_grad, weight_grad)
     return (features.T, input_grad, weight_grad.transpose(2, 0, 1))
 
 

time: 52.4 us -> 80.3 us (1.53)
  Pallas kernels: 46.3 us -> 79.5 us
  local copies, waits for them, and re-layouts: 5.22 us -> 0 us
    pallas_call x0 -> x1, Pallas kernels: none -> 33.6 us  [hand_over(): pl.pallas_call(hand_over_kernel, out_shape=tuple((jax.ShapeDtypeStruct(a....]
    unnamed x3 -> x0, local copies, waits for them, and re-layouts: 5.22 us -> none
where the time goes in v3:
time: 80.3 us; the launch traced here: 80.2 us
  Pallas kernels  79.5 us (99%)
    pallas_call x1, Pallas kernels, per_device(): pl.pallas_call(functools.partial(kernel, n_seq, n_sub, taps), out_shape=(...  45.9 us
    pallas_call x1, Pallas kernels, hand_over(): pl.pallas_call(hand_over_kernel, out_shape=tuple((jax.ShapeDtypeStruct(a....  33.6 us

profile of v3, /device:TPU:1, one launch (start us, length us, event | category | flops | bytes accessed | tf_op | source)
XLA Modules:
  0.0 80.2 jit_solution(14465855201815902323)
XLA Ops:
  0.6 45.9 %shard_map.58 = (bf16[288,128]{1,0:T(8,128)(2,1)}, bf16[128,1024]{1,0:T(8,128)(2,1)}, f32[5,288,128]{2,1,0:T(8,128)}) custom-call(bf16[128,1024]{1,0:T(8,128)(2,1)} %x_hbm.1, bf16[1440,1024]{1,0:T(8,128)(2,1)} %bitcast.4, bf16[288,128]{1,0:T(8,128)(2,1)} %bitcast.6), custom_call_target="tpu_custom_call" | custom-call | flops 2264924160 | bytes 2949120 | tf_op jit(solution)/shard_map/pallas_call | solution.py:493
  46.5 33.6 %shard_map.59 = (bf16[288,128]{1,0:T(8,128)(2,1)}, bf16[128,1024]{1,0:T(8,128)(2,1)}, f32[5,288,128]{2,1,0:T(8,128)}) custom-call(bf16[288,128]{1,0:T(8,128)(2,1)} %get-tuple-element.9.refs_0_, bf16[128,1024]{1,0:T(8,128)(2,1)} %get-tuple-element.10.refs_1_, f32[5,288,128]{2,1,0:T(8,128)} %get-tuple-element.11.refs_2_), custom_call_target="tpu_custom_call" | custom-call | tf_op jit(solution)/shard_map/pallas_call | solution.py:469

commit v4 on v3

--- a/solution.py
+++ b/solution.py
@@ -97,7 +97,7 @@
 
 
 PAD = 16
-VMEM_BYTES = 60 * 1024 * 1024
+VMEM_BYTES = 52 * 1024 * 1024
 F32 = jnp.float32
 BF16 = jnp.bfloat16
 
@@ -469,7 +469,7 @@
     return pl.pallas_call(
         hand_over_kernel,
         out_shape=tuple(jax.ShapeDtypeStruct(a.shape, a.dtype) for a in arrays),
-        in_specs=[hbm] * len(arrays),
+        in_specs=[pl.BlockSpec(memory_space=pltpu.VMEM)] * len(arrays),
         out_specs=(hbm,) * len(arrays),
         scratch_shapes=[pltpu.SemaphoreType.DMA((len(arrays),))],
     )(*arrays)

time: 80.3 us -> 52.5 us (0.65)
  Pallas kernels: 79.5 us -> 47.6 us
  local copies, waits for them, and re-layouts: 0 us -> 4.01 us
    pallas_call x1, Pallas kernels: 33.6 us -> 2.23 us  [hand_over(): pl.pallas_call(hand_over_kernel, out_shape=tuple((jax.ShapeDtypeStruct(a....]
    unnamed x0 -> x10, local copies, waits for them, and re-layouts: none -> 4.01 us
where the time goes in v4:
time: 52.5 us; the launch traced here: 52.2 us
  Pallas kernels  47.6 us (91%)
  local copies, waits for them, and re-layouts  4.01 us (8%)
  between operations  0.66 us (1%)
    pallas_call x1, Pallas kernels, per_device(): pl.pallas_call(functools.partial(kernel, n_seq, n_sub, taps), out_shape=(...  45.3 us
    unnamed x10, local copies, waits for them, and re-layouts  4.01 us
    pallas_call x1, Pallas kernels, hand_over(): pl.pallas_call(hand_over_kernel, out_shape=tuple((jax.ShapeDtypeStruct(a....  2.23 us

profile of v4, /device:TPU:1, one launch (start us, length us, event | category | flops | bytes accessed | tf_op | source)
XLA Modules:
  0.0 52.2 jit_solution(4513149804724853189)
XLA Ops:
  0.6 0.0 copy-start.3
  0.6 0.9 %copy-done.3 = bf16[128,1024]{1,0:T(8,128)(2,1)S(1)} copy-done((bf16[128,1024]{1,0:T(8,128)(2,1)S(1)}, bf16[128,1024]{1,0:T(8,128)(2,1)}, u32[]{:S(2)}) %copy-start.3) | copy-done | bytes 262168
  1.6 0.0 copy-start.4
  1.6 0.9 %copy-done.4 = bf16[128,288]{0,1:T(8,128)(2,1)S(1)} copy-done((bf16[128,288]{0,1:T(8,128)(2,1)S(1)}, bf16[128,288]{0,1:T(8,128)(2,1)}, u32[]{:S(2)}) %copy-start.4) | copy-done | bytes 73752
  2.5 45.3 %shard_map.58 = (bf16[288,128]{1,0:T(8,128)(2,1)S(1)}, bf16[128,1024]{1,0:T(8,128)(2,1)S(1)}, f32[5,288,128]{2,1,0:T(8,128)S(1)}) custom-call(bf16[128,1024]{1,0:T(8,128)(2,1)S(1)} %copy-done.3, bf16[1440,1024]{1,0:T(8,128)(2,1)} %bitcast.5, bf16[288,128]{1,0:T(8,128)(2,1)S(1)} %bitcast.4), custom_call_target="tpu_custom_call" | custom-call | flops 2264924160 | bytes 2949120 | tf_op jit(solution)/shard_map/pallas_call | solution.py:493
  47.8 0.0 copy-start
  47.8 0.9 %copy-done = f32[5,288,128]{2,1,0:T(8,128)} copy-done((f32[5,288,128]{2,1,0:T(8,128)}, f32[5,288,128]{2,1,0:T(8,128)S(1)}, u32[]{:S(2)}) %copy-start) | copy-done | bytes 737304
  48.7 0.0 copy-start.1
  48.7 0.7 %copy-done.1 = bf16[128,1024]{1,0:T(8,128)(2,1)} copy-done((bf16[128,1024]{1,0:T(8,128)(2,1)}, bf16[128,1024]{1,0:T(8,128)(2,1)S(1)}, u32[]{:S(2)}) %copy-start.1) | copy-done | bytes 262168
  49.4 0.0 copy-start.2
  49.4 0.6 %copy-done.2 = bf16[288,128]{1,0:T(8,128)(2,1)} copy-done((bf16[288,128]{1,0:T(8,128)(2,1)}, bf16[288,128]{1,0:T(8,128)(2,1)S(1)}, u32[]{:S(2)}) %copy-start.2) | copy-done | bytes 73752
  50.0 2.2 %shard_map.59 = (bf16[288,128]{1,0:T(8,128)(2,1)}, bf16[128,1024]{1,0:T(8,128)(2,1)}, f32[5,288,128]{2,1,0:T(8,128)}) custom-call(bf16[288,128]{1,0:T(8,128)(2,1)} %copy-done.2, bf16[128,1024]{1,0:T(8,128)(2,1)} %copy-done.1, f32[5,288,128]{2,1,0:T(8,128)} %copy-done), custom_call_target="tpu_custom_call" | custom-call | tf_op jit(solution)/shard_map/pallas_call | solution.py:469
Async XLA Ops:
  0.6 1.0 %copy-start.3 = (bf16[128,1024]{1,0:T(8,128)(2,1)S(1)}, bf16[128,1024]{1,0:T(8,128)(2,1)}, u32[]{:S(2)}) copy-start(bf16[128,1024]{1,0:T(8,128)(2,1)} %x_hbm.1) | copy-start | bytes 786436
  1.6 0.9 %copy-start.4 = (bf16[128,288]{0,1:T(8,128)(2,1)S(1)}, bf16[128,288]{0,1:T(8,128)(2,1)}, u32[]{:S(2)}) copy-start(bf16[128,288]{0,1:T(8,128)(2,1)} %param.5) | copy-start | bytes 221188
  47.8 0.9 %copy-start = (f32[5,288,128]{2,1,0:T(8,128)}, f32[5,288,128]{2,1,0:T(8,128)S(1)}, u32[]{:S(2)}) copy-start(f32[5,288,128]{2,1,0:T(8,128)S(1)} %get-tuple-element.11.refs_2_) | copy-start | bytes 2211844
  48.7 0.7 %copy-start.1 = (bf16[128,1024]{1,0:T(8,128)(2,1)}, bf16[128,1024]{1,0:T(8,128)(2,1)S(1)}, u32[]{:S(2)}) copy-start(bf16[128,1024]{1,0:T(8,128)(2,1)S(1)} %get-tuple-element.10.refs_1_) | copy-start | bytes 786436
  49.4 0.6 %copy-start.2 = (bf16[288,128]{1,0:T(8,128)(2,1)}, bf16[288,128]{1,0:T(8,128)(2,1)S(1)}, u32[]{:S(2)}) copy-start(bf16[288,128]{1,0:T(8,128)(2,1)S(1)} %get-tuple-element.9.refs_0_) | copy-start | bytes 221188
